TPU v7x, 32 devices: a whole 2x2x4 slice. The times are simulated.
32 devices in a mesh: parts: 2 (over y), dp: 8 (over z, x), fac: 2 (over core).
Axes of the slice: x: 2, y: 2, z: 4, core: 2. Of those that a mesh axis runs over, the one named last changes fastest.
Arguments:
- acts: bfloat16 [2816, 14336], P(('parts', 'dp'), 'fac'), parts along dimension 0, may hold values from -6 to 6
- grads: bfloat16 [2816, 4096], P(('parts', 'dp'), 'fac'), parts along dimension 0, may hold values from -6 to 6
- lengths: int32 [16, 4], P(('parts', 'dp')), parts along dimension 0, may hold values from 1 to 88, 176 in all within a row
- basis_a: bfloat16 [2, 7168, 14336], P('fac', 'dp'), may hold values from -0.046875 to 0.046875
- basis_g: bfloat16 [2, 2048, 4096], P('fac', 'dp'), may hold values from -0.09375 to 0.09375
- coef_a: bfloat16 [14336, 256], P(('dp', 'fac')), may hold values from -0.009765625 to 0.009765625
- coef_g: bfloat16 [4096, 256], P(('dp', 'fac')), may hold values from -0.01953125 to 0.01953125
- eig_a: float32 [14336], P(('dp', 'fac')), may hold values from 0.02 to 2
- eig_g: float32 [4096], P(('dp', 'fac')), may hold values from 0.02 to 2
Outputs:
- scores: float32 [64, 8], P(('parts', 'dp'), 'fac'), parts along dimension 0
There are 2 independent parts, one for each index of `parts`. A program takes and returns all parts, laid end to end along the dimension named above; an argument that names none is the same for every part. Nothing has to cross between parts.
Inputs may be any that keep to these rules, and one draw needn't show every extreme that they name: `lengths`: in each index of dp the counts sum to 176, and the largest of them is exactly 88.
All inputs are finite; a program needn't handle non-finite values.
Results may differ from a plain program's by a relative error of at most 0.0057.
Values may be sent and summed in bfloat16 or wider, within the bound.
A program may use at most 128 MiB of HBM per device.

v0:
```python
import jax
import jax.numpy as jnp
from jax import lax
from jax.sharding import PartitionSpec as P

RANK = 32


damping = 0.1


def on_device(acts, grads, lengths, basis_a, basis_g, coef_a, coef_g, eig_a, eig_g):
    scaled_a = (coef_a.astype(jnp.float32) / (eig_a[:, None] + damping)).astype(jnp.bfloat16)
    scaled_g = (coef_g.astype(jnp.float32) / (eig_g[:, None] + damping)).astype(jnp.bfloat16)
    panel_a = basis_a[0]
    panel_g = basis_g[0]
    query_cols = scaled_a.shape[1]
    coef_rows_a = scaled_a.shape[0]
    coef_rows_g = scaled_g.shape[0]
    coef_rows = coef_rows_a + coef_rows_g
    coef_stack = jnp.concatenate([scaled_a, scaled_g], axis=0)
    section = lax.all_gather(coef_stack, ("dp", "fac"), axis=0, tiled=True)
    shard_count = section.shape[0] // coef_rows
    blocks = section.reshape(shard_count, coef_rows, query_cols)
    part_a = blocks[:, :coef_rows_a].reshape(shard_count * coef_rows_a, query_cols)
    part_g = blocks[:, coef_rows_a:].reshape(shard_count * coef_rows_g, query_cols)
    summed_a = jnp.dot(panel_a, part_a, preferred_element_type=jnp.float32)
    summed_g = jnp.dot(panel_g, part_g, preferred_element_type=jnp.float32)
    factor_a = summed_a.astype(jnp.bfloat16)
    factor_g = summed_g.astype(jnp.bfloat16)
    tok_rows = acts.shape[0]
    columns = acts
    proj_a = jnp.dot(
        columns,
        lax.all_gather(factor_a, "dp", axis=0, tiled=True),
        preferred_element_type=jnp.float32,
    )
    columns = grads
    proj_g = jnp.dot(
        columns,
        lax.all_gather(factor_g, "dp", axis=0, tiled=True),
        preferred_element_type=jnp.float32,
    )
    share_a, share_g = (
        lax.psum_scatter(proj_a, "fac", scatter_dimension=1, tiled=True),
        lax.psum_scatter(proj_g, "fac", scatter_dimension=1, tiled=True),
    )
    owned_queries = share_a.shape[1] // RANK
    products = (share_a * share_g).reshape(tok_rows, owned_queries, RANK).sum(axis=2)
    counts = lengths[0]
    doc_ends = jnp.cumsum(counts)
    doc_starts = doc_ends - counts
    position = jnp.arange(tok_rows, dtype=jnp.int32)
    member = (
        (position[:, None] >= doc_starts[None, :]) & (position[:, None] < doc_ends[None, :])
    ).astype(jnp.float32)
    sums = jnp.einsum("td,tq->dq", member, products, precision=lax.Precision.HIGHEST)
    divisor = jnp.sqrt(RANK * counts.astype(jnp.float32))
    return sums / divisor[:, None]


def solution(mesh):
    placed = (
        P(("parts", "dp"), "fac"),
        P(("parts", "dp"), "fac"),
        P(("parts", "dp"), None),
        P("fac", "dp", None),
        P("fac", "dp", None),
        P(("dp", "fac"), None),
        P(("dp", "fac"), None),
        P(("dp", "fac")),
        P(("dp", "fac")),
    )
    return jax.shard_map(
        on_device, mesh=mesh, in_specs=placed, out_specs=P(("parts", "dp"), "fac"), check_vma=False
    )
```

profile of v0, /device:TPU:1, one launch (start us, length us, event | category | flops | bytes accessed | tf_op | source)
XLA Modules:
  0.0 238.6 jit_solution(3814409713334278510)
XLA Ops:
  6.5 0.8 broadcast_add_fusion
  7.4 0.7 broadcast_add_fusion.1
  8.1 1.2 divide_convert_fusion
  9.3 1.0 divide_convert_fusion.1
  10.3 0.9 pad_maximum_fusion
  11.2 0.0 all-gather.8.cloned.1.call-start
  11.2 84.1 %all-gather.4.cloned.1.call-done = bf16[18432,256]{1,0:T(8,128)(2,1)} async-done(((bf16[1152,256]{1,0:T(8,128)(2,1)}), bf16[18432,256]{1,0:T(8,128)(2,1)}) %all-gather.4.cloned.1.call-update) | async-done | bytes 9437200 | tf_op jit(solution)/shard_map/all_gather | solution.py:22
  95.3 6.6 %slice.8 = bf16[16,896,256]{2,1,0:T(8,128)(2,1)} slice(bf16[16,1152,256]{2,1,0:T(8,128)(2,1)} %bitcast.44), slice={[0:16], [0:896], [0:256]} | slice | bytes 14680064 | tf_op jit(solution)/shard_map/slice | solution.py:25
  101.9 1.9 slice.9
  103.8 0.3 copy-done.2
  104.1 1.4 fusion.13
  105.6 0.0 all-gather.6.cloned.1.call-start
  105.6 15.5 %fusion.7 = bf16[896,256]{0,1:T(8,128)(2,1)} fusion(bf16[14336,256]{1,0:T(8,128)(2,1)} %bitcast.46, bf16[1,896,14336]{2,1,0:T(8,128)(2,1)} %param.12), kind=kOutput, calls=%fused_computation.5 | convolution fusion | flops 6576898048 | bytes 33488896 | tf_op jit(solution)/shard_map/dot_general | solution.py:27
  121.2 0.0 reduce-scatter.5.cloned.1.call-start
  121.3 0.2 reduce-window.4
  121.4 19.1 %all-gather.8.cloned.1.call-done = bf16[2048,256]{0,1:T(8,128)(2,1)} async-done(((bf16[256,256]{0,1:T(8,128)(2,1)}), bf16[2048,256]{0,1:T(8,128)(2,1)}) %all-gather.8.cloned.1.call-update) | async-done | bytes 1048592 | tf_op jit(solution)/shard_map/all_gather | solution.py:41
  140.5 2.4 %convolution_bitcast_fusion = f32[176,256]{1,0:T(8,128)} fusion(bf16[2048,256]{0,1:T(8,128)(2,1)} %all-gather.8.cloned.1.call-done, bf16[176,2048]{1,0:T(8,128)(2,1)S(1)} %copy-done.1), kind=kOutput, calls=%fused_computation.7 | convolution fusion | flops 184549376 | bytes 1949696 | tf_op jit(solution)/shard_map/dot_general | solution.py:39
  143.0 67.0 %all-gather.6.cloned.1.call-done = bf16[7168,256]{0,1:T(8,128)(2,1)} async-done(((bf16[896,256]{0,1:T(8,128)(2,1)}), bf16[7168,256]{0,1:T(8,128)(2,1)}) %all-gather.6.cloned.1.call-update) | async-done | bytes 3670032 | tf_op jit(solution)/shard_map/all_gather | solution.py:35
  210.1 4.1 %convolution_bitcast_fusion.1 = f32[176,256]{1,0:T(8,128)} fusion(bf16[7168,256]{0,1:T(8,128)(2,1)} %all-gather.6.cloned.1.call-done, bf16[176,7168]{1,0:T(8,128)(2,1)S(1)} %copy-done), kind=kOutput, calls=%fused_computation.8 | convolution fusion | flops 645922816 | bytes 6373376 | tf_op jit(solution)/shard_map/dot_general | solution.py:33
  214.2 5.2 %reduce-scatter.5.cloned.1.call-done = f32[176,128]{1,0:T(8,128)} async-done(((f32[176,256]{1,0:T(8,128)}), f32[176,128]{1,0:T(8,128)}) %reduce-scatter.5.cloned.1.call-update) | async-done | bytes 90128 | tf_op jit(solution)/shard_map/reduce_scatter | solution.py:46
  219.4 10.8 %reduce-scatter.3.cloned.1.call-done = f32[176,128]{1,0:T(8,128)} async-done(((f32[176,256]{1,0:T(8,128)}), f32[176,128]{1,0:T(8,128)}) %reduce-scatter.3.cloned.1.call-update) | async-done | bytes 90128 | tf_op jit(solution)/shard_map/reduce_scatter | solution.py:45
  230.2 0.9 mul.11
  231.1 0.1 copy.11
  231.3 0.8 convolution_divide_fusion
  (17 shorter events, 0.2 us)
Async XLA Ops:
  6.5 203.5 %copy-start = (bf16[176,7168]{1,0:T(8,128)(2,1)S(1)}, bf16[176,7168]{1,0:T(8,128)(2,1)}, u32[]{:S(2)}) copy-start(bf16[176,7168]{1,0:T(8,128)(2,1)} %param.9) | copy-start | bytes 7569412
  6.5 88.7 %all-gather.4.cloned.1.call-start = ((), (), s32[]{:S(2)}) async-start(), calls=%async_computation.2 | async-start | bytes 10027008 | tf_op jit(solution)/shard_map/all_gather | solution.py:22
  11.2 129.4 %all-gather.8.cloned.1.call-start = ((), (), s32[]{:S(2)}) async-start(), calls=%async_computation.5 | async-start | bytes 1179648 | tf_op jit(solution)/shard_map/all_gather | solution.py:41
  101.9 2.2 copy-start.2
  105.6 104.5 %all-gather.6.cloned.1.call-start = ((), (), s32[]{:S(2)}) async-start(), calls=%async_computation.3 | async-start | bytes 4128768 | tf_op jit(solution)/shard_map/all_gather | solution.py:35
  105.6 15.6 %copy-start.3 = (s32[1,4]{1,0:T(1,128)S(1)}, s32[1,4]{1,0:T(1,128)}, u32[]{:S(2)}) copy-start(s32[1,4]{1,0:T(1,128)} %param.11) | copy-start | bytes 52
  105.6 34.9 %copy-start.1 = (bf16[176,2048]{1,0:T(8,128)(2,1)S(1)}, bf16[176,2048]{1,0:T(8,128)(2,1)}, u32[]{:S(2)}) copy-start(bf16[176,2048]{1,0:T(8,128)(2,1)} %param.10) | copy-start | bytes 2162692
  121.2 98.2 %reduce-scatter.5.cloned.1.call-start = ((), (), s32[]{:S(2)}) async-start(), calls=%async_computation.6 | async-start | bytes 270336 | tf_op jit(solution)/shard_map/reduce_scatter | solution.py:46
  143.0 87.2 %reduce-scatter.3.cloned.1.call-start = ((), (), s32[]{:S(2)}) async-start(), calls=%async_computation.4 | async-start | bytes 270336 | tf_op jit(solution)/shard_map/reduce_scatter | solution.py:45
Sparse Core Ops, SparseCore 0:
  11.3 83.9 all-gather.3
  105.7 34.8 all-gather.7
  142.7 67.2 all-gather.5
  212.1 7.2 reduce-scatter.4
  221.5 8.6 reduce-scatter.2
where the time goes:
time: 239 us
  waiting for transfers between devices  186 us (78%)
  matrix products  24.2 us (10%)
  between operations  13.2 us (6%)
  local copies, waits for them, and re-layouts  8.97 us (4%)
  other arithmetic  5.76 us (2%)
    all_gather x1, waiting for transfers between devices, on_device(): section = lax.all_gather(coef_stack, ('dp', 'fac'), axis=0, tiled=True)  84.1 us
    all_gather x1, waiting for transfers between devices, on_device(): lax.all_gather(factor_a, 'dp', axis=0, tiled=True)  67 us
    all_gather x1, waiting for transfers between devices, on_device(): lax.all_gather(factor_g, 'dp', axis=0, tiled=True)  19.1 us
    dot_general x1, matrix products, on_device(): summed_a = jnp.dot(panel_a, part_a, preferred_element_type=jnp.float32)  15.5 us
    reduce_scatter x1, waiting for transfers between devices, on_device(): lax.psum_scatter(proj_a, 'fac', scatter_dimension=1, tiled=True)  10.8 us
    slice x1, local copies, waits for them, and re-layouts, on_device(): blocks[:, :coef_rows_a].reshape(shard_count * coef_rows_a, query_cols)  6.64 us
    reduce_scatter x1, waiting for transfers between devices, on_device(): lax.psum_scatter(proj_g, 'fac', scatter_dimension=1, tiled=True)  5.21 us
  transfers between devices with their start and end apart: 5, of which 5 were waited for; matrix products, arithmetic and copies ran while one was open for 9% of the time, Pallas kernels for 0%

commit v1 on v0

v1 whole, which is shorter than its diff:
```python
import functools

import jax
import jax.numpy as jnp
from jax import lax
from jax.experimental import pallas as pl
from jax.experimental.pallas import tpu as pltpu
from jax.sharding import PartitionSpec as P

RANK = 32
LANES = 128


damping = 0.1


def scaled(coef, eig):
    return (coef.astype(jnp.float32) / (eig[:, None] + damping)).astype(jnp.bfloat16)


def on_device(acts, grads, lengths, basis_a, basis_g, coef_a, coef_g, eig_a, eig_g):
    scaled_a = scaled(coef_a, eig_a)
    scaled_g = scaled(coef_g, eig_g)
    part_a = lax.all_gather(scaled_a, ("dp", "fac"), axis=0, tiled=True)
    part_g = lax.all_gather(scaled_g, ("dp", "fac"), axis=0, tiled=True)
    factor_a = jnp.dot(basis_a[0], part_a, preferred_element_type=jnp.float32).astype(jnp.bfloat16)
    factor_g = jnp.dot(basis_g[0], part_g, preferred_element_type=jnp.float32).astype(jnp.bfloat16)
    proj_a = jnp.dot(
        acts,
        lax.all_gather(factor_a, "dp", axis=0, tiled=True),
        preferred_element_type=jnp.float32,
    )
    proj_g = jnp.dot(
        grads,
        lax.all_gather(factor_g, "dp", axis=0, tiled=True),
        preferred_element_type=jnp.float32,
    )
    share_a = lax.psum_scatter(proj_a, "fac", scatter_dimension=1, tiled=True)
    share_g = lax.psum_scatter(proj_g, "fac", scatter_dimension=1, tiled=True)
    tok_rows = acts.shape[0]
    owned_queries = share_a.shape[1] // RANK
    products = (share_a * share_g).reshape(tok_rows, owned_queries, RANK).sum(axis=2)
    counts = lengths[0]
    docs = counts.shape[0]
    before = jnp.arange(docs)[:, None] <= jnp.arange(docs)[None, :]
    doc_ends = jnp.sum(jnp.where(before, counts[:, None], 0), axis=0)
    doc_starts = doc_ends - counts
    position = jnp.arange(tok_rows, dtype=jnp.int32)
    member = (
        (position[:, None] >= doc_starts[None, :]) & (position[:, None] < doc_ends[None, :])
    ).astype(jnp.float32)
    sums = jnp.einsum("td,tq->dq", member, products, precision=lax.Precision.HIGHEST)
    divisor = jnp.sqrt(RANK * counts.astype(jnp.float32))
    return sums / divisor[:, None]


def kernel(
    dims, len_ref, stack, acts, grads, basis_a, basis_g, out,
    coefs, panel_a, panel_g, sum_a, sum_g, give, facs, padded, toks_a, toks_g,
    proj, from_sib, to_y, from_y,
    pa_sem, pg_sem, own_sem,
    line1_s, line1_r, x1_s, x1_r, sib_s, sib_r,
    line2_s, line2_r, x2_s, x2_r, y_s, y_r,
    ta_l, ta_s, ta_r, tg_l, tg_s, tg_r, end_s, end_r,
):
    nz, nx, rows_a, rows_g, docs = dims
    p, d, f = lax.axis_index("parts"), lax.axis_index("dp"), lax.axis_index("fac")
    z, x = d // nx, d % nx
    nd = nz * nx
    half_a, half_g = rows_a // 2, rows_g // 2
    wide = toks_a.shape[3]
    tok_rows = acts.shape[0]

    def dev(pp=None, zz=None, xx=None, ff=None):
        zz = z if zz is None else zz
        xx = x if xx is None else xx
        return (p if pp is None else pp, zz * nx + xx, f if ff is None else ff)

    def send(src, dst, s, r, where):
        return pltpu.make_async_remote_copy(
            src_ref=src, dst_ref=dst, send_sem=s, recv_sem=r,
            device_id=where, device_id_type=pl.DeviceIdType.MESH,
        )

    deep = nx * 2 * rows_a

    def load_panel(zb):
        return pltpu.make_async_copy(
            basis_a.at[0, :, pl.ds(pl.multiple_of(zb * deep, LANES), deep)],
            panel_a.at[zb], pa_sem.at[zb],
        )

    load_g = pltpu.make_async_copy(basis_g.at[0], panel_g, pg_sem)
    own = pltpu.make_async_copy(
        stack.at[:, pl.ds(pl.multiple_of(p * LANES, LANES), LANES)], coefs.at[z, x, f], own_sem
    )
    own.start()
    load_g.start()
    for s in range(nz):
        load_panel(lax.rem(z + s, nz)).start()

    barrier = pltpu.get_barrier_semaphore()
    for where in (dev(pp=1 - p), dev(pp=1 - p, ff=1 - f), dev(ff=1 - f), dev(xx=1 - x)):
        pl.semaphore_signal(barrier, inc=1, device_id=where, device_id_type=pl.DeviceIdType.MESH)

    @pl.when(z > 0)
    def _():
        pl.semaphore_signal(
            barrier, inc=1, device_id=dev(zz=z - 1), device_id_type=pl.DeviceIdType.MESH
        )

    @pl.when(z < nz - 1)
    def _():
        pl.semaphore_signal(
            barrier, inc=1, device_id=dev(zz=z + 1), device_id_type=pl.DeviceIdType.MESH
        )

    pl.semaphore_wait(barrier, 4 + jnp.where(z > 0, 1, 0) + jnp.where(z < nz - 1, 1, 0))
    own.wait()

    def line(block, ss, rr, up, step):
        zb = z - (step - 1) if up else z + (step - 1)
        k = 0 if up else 1
        return send(block(zb, x), block(zb, x), ss.at[k, step], rr.at[k, step],
                    dev(zz=z + 1 if up else z - 1))

    def landed(block, ss, rr, up, step):
        zb = z - step if up else z + step
        k = 0 if up else 1
        return send(block(zb, x), block(zb, x), ss.at[k, step], rr.at[k, step],
                    dev(zz=z - 1 if up else z + 1))

    def across(block, ss, rr, zb, xb):
        return send(block(zb, xb), block(zb, xb), ss.at[zb], rr.at[zb], dev(xx=1 - x))

    def twin(zb, xb, ff):
        return send(coefs.at[zb, xb, ff], coefs.at[zb, xb, ff],
                    sib_s.at[zb, xb], sib_r.at[zb, xb], dev(ff=1 - f))

    def gather(block, ls, lr, xs, xr, extra, use):
        def pass_on(zb):
            across(block, xs, xr, zb, x).start()
            extra(zb, x)

        @pl.when(z < nz - 1)
        def _():
            line(block, ls, lr, True, 1).start()

        @pl.when(z > 0)
        def _():
            line(block, ls, lr, False, 1).start()

        pass_on(z)

        def step(s, carry):
            @pl.when((s < nz) & (z - s >= 0))
            def _():
                landed(block, ls, lr, True, s).wait_recv()

                @pl.when(z < nz - 1)
                def _():
                    line(block, ls, lr, True, s + 1).start()

                pass_on(z - s)

            @pl.when((s < nz) & (z + s < nz))
            def _():
                landed(block, ls, lr, False, s).wait_recv()

                @pl.when(z > 0)
                def _():
                    line(block, ls, lr, False, s + 1).start()

                pass_on(z + s)

            def side(j, c):
                zb = z + (s - 1) * (2 * j - 1)

                @pl.when((zb >= 0) & (zb < nz) & ((s > 1) | (j == 0)))
                def _():
                    across(block, xs, xr, zb, 1 - x).wait_recv()
                    extra(zb, 1 - x)
                    use(zb)

                return c

            return lax.fori_loop(0, 2, side, carry)

        lax.fori_loop(1, nz + 1, step, 0)

    def gather_sent(block, ls, lr, xs, xr):
        def step(s, carry):
            @pl.when((z < nz - 1) & (z - s + 1 >= 0))
            def _():
                line(block, ls, lr, True, s).wait_send()

            @pl.when((z > 0) & (z + s - 1 < nz))
            def _():
                line(block, ls, lr, False, s).wait_send()

            return carry

        lax.fori_loop(1, nz, step, 0)

        def crossing(zb, carry):
            across(block, xs, xr, zb, x).wait_send()
            return carry

        lax.fori_loop(0, nz, crossing, 0)

    step_a = rows_a - wide

    def cols_a(db, q):
        return pl.ds(pl.multiple_of(db * rows_a + q * step_a, LANES), wide)

    def cols_g(db, q):
        return pl.ds(pl.multiple_of(db * rows_g + q * half_g, LANES), half_g)

    def own_a(db):
        return pltpu.make_async_copy(acts.at[:, cols_a(db, p)], toks_a.at[p, db], ta_l.at[db])

    def own_g(db):
        return pltpu.make_async_copy(grads.at[:, cols_g(db, p)], toks_g.at[p, db], tg_l.at[db])

    def swap_a(db, q):
        return send(acts.at[:, cols_a(db, 1 - p)], toks_a.at[q, db], ta_s.at[db], ta_r.at[db],
                    dev(pp=1 - p))

    def swap_g(db, q):
        return send(grads.at[:, cols_g(db, 1 - p)], toks_g.at[q, db], tg_s.at[db], tg_r.at[db],
                    dev(pp=1 - p))

    early = (nd + 1) // 2

    def start_swaps(lo, hi):
        def body(db, carry):
            swap_a(db, p).start()
            swap_g(db, p).start()
            return carry

        lax.fori_loop(lo, hi, body, 0)

    def block1(zb, xb):
        return coefs.at[zb, xb, f]

    def extra1(zb, xb):
        twin(zb, xb, f).start()

    sum_a[...] = jnp.zeros_like(sum_a)
    sum_g[...] = jnp.zeros_like(sum_g)
    padded[...] = jnp.zeros_like(padded)
    proj[...] = jnp.zeros_like(proj)

    def use1(zb):
        load_panel(zb).wait()

        @pl.when(zb == z)
        def _():
            load_g.wait()

        for xb in range(nx):
            twin(zb, xb, 1 - f).wait_recv()
        total_a, total_g = sum_a[...], sum_g[...]
        for i in range(nx * 2):
            block = coefs.at[zb, i // 2, i % 2]
            total_a += jnp.dot(
                panel_a[zb, :, i * rows_a:(i + 1) * rows_a], block[:rows_a],
                preferred_element_type=jnp.float32,
            )
            at = pl.multiple_of((zb * nx * 2 + i) * rows_g, LANES)
            total_g += jnp.dot(
                panel_g[:, pl.ds(at, rows_g)], block[rows_a:],
                preferred_element_type=jnp.float32,
            )
        sum_a[...] = total_a
        sum_g[...] = total_g

    start_swaps(0, early)

    def start_own(db, carry):
        own_a(db).start()
        own_g(db).start()
        return carry

    lax.fori_loop(0, nd, start_own, 0)
    gather(block1, line1_s, line1_r, x1_s, x1_r, extra1, use1)

    def halves(q):
        return (
            sum_a[pl.ds(pl.multiple_of(q * half_a, 16), half_a), :].astype(jnp.bfloat16),
            sum_g[pl.ds(pl.multiple_of(q * half_g, 16), half_g), :].astype(jnp.bfloat16),
        )

    give_a, give_g = halves(1 - p)
    give[:half_a] = give_a
    give[half_a:] = give_g
    send(give, facs.at[z, x, p], y_s, y_r, dev(pp=1 - p)).start()
    keep_a, keep_g = halves(p)
    facs[z, x, p, :half_a] = keep_a
    facs[z, x, p, half_a:] = keep_g
    start_swaps(early, nd)
    send(give, facs.at[z, x, 1 - p], y_s, y_r, dev(pp=1 - p)).wait()

    def block2(zb, xb):
        return facs.at[zb, xb]

    lead = half_a - step_a

    def use2(zb):
        for xb in range(nx):
            db = zb * nx + xb
            own_a(db).wait()
            own_g(db).wait()
            swap_a(db, 1 - p).wait_recv()
            swap_g(db, 1 - p).wait_recv()
            rows = pl.ds(pl.multiple_of(p * lead, 16), half_a)
            for c in range(2):
                padded[rows, c * LANES:(c + 1) * LANES] = facs[zb, xb, c, :half_a]
            fac_g = jnp.concatenate([facs[zb, xb, c, half_a:] for c in range(2)], axis=1)
            fac_a = padded[...]
            for q in range(2):
                proj[0, q] += jnp.dot(toks_a[q, db], fac_a, preferred_element_type=jnp.float32)
                proj[1, q] += jnp.dot(toks_g[q, db], fac_g, preferred_element_type=jnp.float32)

    gather(block2, line2_s, line2_r, x2_s, x2_r, lambda zb, xb: None, use2)

    def half(q):
        return pl.ds(pl.multiple_of(q * LANES, LANES), LANES)

    for ff in range(2):
        to_y[ff] = proj[:, 1 - p, :, ff * LANES:(ff + 1) * LANES].astype(jnp.bfloat16)
    ends = [
        send(to_y.at[f], from_y.at[f], end_s.at[0], end_r.at[0], dev(pp=1 - p)),
        send(to_y.at[1 - f], from_y.at[f], end_s.at[1], end_r.at[1], dev(pp=1 - p, ff=1 - f)),
        send(proj.at[:, p, :, half(1 - f)], from_sib, end_s.at[2], end_r.at[2], dev(ff=1 - f)),
    ]
    for copy in ends:
        copy.start()

    counts = [len_ref[0, i] for i in range(docs)]
    row = lax.broadcasted_iota(jnp.int32, (8, tok_rows), 0)
    position = lax.broadcasted_iota(jnp.int32, (8, tok_rows), 1)
    doc = lax.broadcasted_iota(jnp.int32, (8, LANES), 0)
    member = jnp.zeros((8, tok_rows), jnp.float32)
    size = jnp.ones((8, LANES), jnp.float32)
    begin = jnp.int32(0)
    for i in range(docs):
        stop = begin + counts[i]
        inside = (row == i) & (position >= begin) & (position < stop)
        member = jnp.where(inside, 1.0, member)
        size = jnp.where(doc == i, counts[i].astype(jnp.float32), size)
        begin = stop
    column = lax.broadcasted_iota(jnp.int32, (LANES, LANES), 0)
    query = lax.broadcasted_iota(jnp.int32, (LANES, LANES), 1)
    same = ((column >= query * RANK) & (column < (query + 1) * RANK)).astype(jnp.float32)

    send(to_y.at[f], from_y.at[f], end_s.at[0], end_r.at[0], dev(pp=1 - p)).wait_recv()
    send(to_y.at[f], from_y.at[1 - f], end_s.at[1], end_r.at[1], dev(pp=1 - p)).wait_recv()
    ends[2].wait_recv()
    total = (
        proj[:, p, :, half(f)] + from_sib[...]
        + from_y[0].astype(jnp.float32) + from_y[1].astype(jnp.float32)
    )
    exact = dict(precision=lax.Precision.HIGHEST, preferred_element_type=jnp.float32)
    sums = jnp.dot(jnp.dot(member, total[0] * total[1], **exact), same, **exact)
    sums = sums / jnp.sqrt(RANK * size)
    out[...] = sums[:out.shape[0], :out.shape[1]]

    gather_sent(block1, line1_s, line1_r, x1_s, x1_r)
    gather_sent(block2, line2_s, line2_r, x2_s, x2_r)

    def twins(db, carry):
        twin(db // nx, db % nx, f).wait_send()
        return carry

    lax.fori_loop(0, nd, twins, 0)

    def swaps(db, carry):
        swap_a(db, p).wait_send()
        swap_g(db, p).wait_send()
        return carry

    lax.fori_loop(0, nd, swaps, 0)
    for copy in ends:
        copy.wait_send()


def with_kernel(nz, nx, acts, grads, lengths, basis_a, basis_g, coef_a, coef_g, eig_a, eig_g):
    stack = jnp.concatenate([scaled(coef_a, eig_a), scaled(coef_g, eig_g)], axis=0)
    rows_a, rows_g = basis_a.shape[1], basis_g.shape[1]
    tok_rows, docs = acts.shape[0], lengths.shape[1]
    nd = nz * nx
    half_a, half_g = rows_a // 2, rows_g // 2
    wide = -(-half_a // LANES) * LANES
    owned = coef_a.shape[1] // 2 // RANK
    bf, f32, dma = jnp.bfloat16, jnp.float32, pltpu.SemaphoreType.DMA
    vmem = pltpu.VMEM
    anywhere = pl.BlockSpec(memory_space=pl.ANY)
    return pl.pallas_call(
        functools.partial(kernel, (nz, nx, rows_a, rows_g, docs)),
        out_shape=jax.ShapeDtypeStruct((docs, owned), f32),
        in_specs=[
            pl.BlockSpec(memory_space=pltpu.SMEM), pl.BlockSpec(memory_space=vmem),
            anywhere, anywhere, anywhere, anywhere,
        ],
        out_specs=pl.BlockSpec(memory_space=vmem),
        scratch_shapes=[
            vmem((nz, nx, 2, rows_a + rows_g, LANES), bf),
            vmem((nz, rows_a, nx * 2 * rows_a), bf),
            vmem(basis_g.shape[1:], bf),
            vmem((rows_a, LANES), f32),
            vmem((rows_g, LANES), f32),
            vmem((half_a + half_g, LANES), bf),
            vmem((nz, nx, 2, half_a + half_g, LANES), bf),
            vmem((wide, 2 * LANES), bf),
            vmem((2, nd, tok_rows, wide), bf),
            vmem((2, nd, tok_rows, half_g), bf),
            vmem((2, 2, tok_rows, 2 * LANES), f32),
            vmem((2, tok_rows, LANES), f32),
            vmem((2, 2, tok_rows, LANES), bf),
            vmem((2, 2, tok_rows, LANES), bf),
            dma((nz,)), dma, dma,
            dma((2, nz + 1)), dma((2, nz + 1)), dma((nz,)), dma((nz,)), dma((nz, nx)), dma((nz, nx)),
            dma((2, nz + 1)), dma((2, nz + 1)), dma((nz,)), dma((nz,)), dma, dma,
            dma((nd,)), dma((nd,)), dma((nd,)), dma((nd,)), dma((nd,)), dma((nd,)),
            dma((3,)), dma((3,)),
        ],
        compiler_params=pltpu.CompilerParams(
            collective_id=0, has_side_effects=True, vmem_limit_bytes=56 * 2**20
        ),
        cost_estimate=pl.CostEstimate(
            flops=2 * rows_a * basis_a.shape[2] * LANES, transcendentals=0,
            bytes_accessed=2 * basis_a.size,
        ),
    )(lengths, stack, acts, grads, basis_a, basis_g)


def chosen(sizes, *arrays):
    acts, grads, lengths, basis_a, basis_g, coef_a = arrays[:6]
    rows_a, rows_g = basis_a.shape[1], basis_g.shape[1]
    nx = 2
    fits = (
        sizes["parts"] == 2 and sizes["fac"] == 2 and sizes["dp"] % nx == 0
        and coef_a.shape[1] == 2 * LANES
        and rows_a % LANES == 0 and rows_g % (2 * LANES) == 0 and acts.shape[0] % 16 == 0
        and coef_a.shape[0] == rows_a and lengths.shape[1] <= 8
    )
    if not fits:
        return on_device(*arrays)
    return with_kernel(sizes["dp"] // nx, nx, *arrays)


def solution(mesh):
    placed = (
        P(("parts", "dp"), "fac"),
        P(("parts", "dp"), "fac"),
        P(("parts", "dp"), None),
        P("fac", "dp", None),
        P("fac", "dp", None),
        P(("dp", "fac"), None),
        P(("dp", "fac"), None),
        P(("dp", "fac")),
        P(("dp", "fac")),
    )
    return jax.shard_map(
        functools.partial(chosen, dict(mesh.shape)),
        mesh=mesh, in_specs=placed, out_specs=P(("parts", "dp"), "fac"), check_vma=False,
    )
```

time: 239 us -> 88.3 us (0.37)
  waiting for transfers between devices: 186 us -> 0 us
  Pallas kernels: 0 us -> 82.3 us
  matrix products: 24.2 us -> 0 us
  between operations: 13.2 us -> 0.03 us
  local copies, waits for them, and re-layouts: 8.97 us -> 1.26 us
    all_gather x3 -> x0, waiting for transfers between devices: 170 us -> none  [the longest x1 84.1 us: on_device(): section = lax.all_gather(coef_stack, ('dp', 'fac'), axis=0, tiled=True)]
    pallas_call x0 -> x1, Pallas kernels: none -> 82.3 us  [with_kernel(): pl.pallas_call(functools.partial(kernel, (nz, nx, rows_a, rows_g, docs)),...]
    dot_general x5 -> x0, matrix products: 24.2 us -> none  [the longest x1 15.5 us: on_device(): summed_a = jnp.dot(panel_a, part_a, preferred_element_type=jnp.float32)]
    reduce_scatter x2 -> x0, waiting for transfers between devices: 16 us -> none  [the longest x1 10.8 us: on_device(): lax.psum_scatter(proj_a, 'fac', scatter_dimension=1, tiled=True)]
    slice x2 -> x0, local copies, waits for them, and re-layouts: 8.52 us -> none  [the longest x1 6.64 us: on_device(): blocks[:, :coef_rows_a].reshape(shard_count * coef_rows_a, query_cols)]
  transfers between devices with their start and end apart: 5 -> 0, of which waited for: 5 -> 0; matrix products, arithmetic and copies ran while one was open for 9% -> 0% of each run, Pallas kernels for 0% -> 0%
where the time goes in v1:
time: 88.3 us; the launch traced here: 88 us
  Pallas kernels  82.3 us (93%)
  other arithmetic  4.43 us (5%)
  local copies, waits for them, and re-layouts  1.26 us (1%)
    pallas_call x1, Pallas kernels, with_kernel(): pl.pallas_call(functools.partial(kernel, (nz, nx, rows_a, rows_g, docs)),...  82.3 us
    convert_element_type x2, other arithmetic, scaled(): (coef.astype(jnp.float32) / (eig[:, None] + damping)).astype(jnp.bfloat16)  2.22 us

profile of v1, /device:TPU:1, one launch (start us, length us, event | category | flops | bytes accessed | tf_op | source)
XLA Modules:
  0.0 88.0 jit_solution(4560021704523599640)
XLA Ops:
  0.0 0.7 broadcast_add_fusion.1
  0.7 0.7 broadcast_add_fusion
  1.4 1.0 %divide_convert_fusion.1 = bf16[256,256]{1,0:T(8,128)(2,1)S(1)} fusion(bf16[256,256]{1,0:T(8,128)(2,1)} %param.15, f32[256]{0:T(256)S(1)} %broadcast_add_fusion.1), kind=kLoop, calls=%fused_computation.2 | loop fusion | flops 196608 | bytes 263168 | tf_op jit(solution)/shard_map/convert_element_type | solution.py:18
  2.4 1.2 %divide_convert_fusion = bf16[896,256]{1,0:T(8,128)(2,1)S(1)} fusion(bf16[896,256]{1,0:T(8,128)(2,1)} %param.14, f32[896]{0:T(1024)S(1)} %broadcast_add_fusion), kind=kLoop, calls=%fused_computation | loop fusion | flops 688128 | bytes 921088 | tf_op jit(solution)/shard_map/convert_element_type | solution.py:18
  3.6 0.8 pad_maximum_fusion.stack
  4.5 82.3 %shard_map.91 = f32[4,4]{1,0:T(4,128)} custom-call(s32[1,4]{1,0:T(1,128)} %len_ref.1, bf16[1152,256]{1,0:T(8,128)(2,1)} %pad_maximum_fusion.stack, bf16[176,7168]{1,0:T(8,128)(2,1)} %acts.1, bf16[176,2048]{1,0:T(8,128)(2,1)} %grads.1, bf16[1,896,14336]{2,1,0:T(8,128)(2,1)} %basis_a.1, bf16[1,256,4096]{2,1,0:T(8,128)(2,1)} %basis_g.1), custom_call_target="tpu_custom_call" | custom-call | flops 3288334336 | bytes 25690112 | tf_op jit(solution)/shard_map/pallas_call | solution.py:399
  86.8 1.3 %copy.11 = f32[4,4]{1,0:T(4,128)} copy(f32[4,4]{1,0:T(4,128)} %shard_map.91) | data formatting | bytes 128

commit v2 on v1

--- a/solution.py
+++ b/solution.py
@@ -55,10 +55,10 @@
 
 
 def kernel(
-    dims, len_ref, stack, acts, grads, basis_a, basis_g, out,
+    dims, len_ref, coef_a, coef_g, eig_a, eig_g, acts, grads, basis_a, basis_g, out,
     coefs, panel_a, panel_g, sum_a, sum_g, give, facs, padded, toks_a, toks_g,
     proj, from_sib, to_y, from_y,
-    pa_sem, pg_sem, own_sem,
+    pa_sem, pg_sem,
     line1_s, line1_r, x1_s, x1_r, sib_s, sib_r,
     line2_s, line2_r, x2_s, x2_r, y_s, y_r,
     ta_l, ta_s, ta_r, tg_l, tg_s, tg_r, end_s, end_r,
@@ -91,13 +91,17 @@
         )
 
     load_g = pltpu.make_async_copy(basis_g.at[0], panel_g, pg_sem)
-    own = pltpu.make_async_copy(
-        stack.at[:, pl.ds(pl.multiple_of(p * LANES, LANES), LANES)], coefs.at[z, x, f], own_sem
-    )
-    own.start()
     load_g.start()
     for s in range(nz):
         load_panel(lax.rem(z + s, nz)).start()
+
+    def scale(coef, eig, first):
+        for at in range(0, coef.shape[0], LANES):
+            divisor = jnp.broadcast_to(eig[pl.ds(at, LANES)][None, :] + damping, (LANES, LANES)).T
+            rows = coef[at:at + LANES, pl.ds(pl.multiple_of(p * LANES, LANES), LANES)]
+            coefs[z, x, f, first + at:first + at + LANES] = (
+                rows.astype(jnp.float32) / divisor
+            ).astype(jnp.bfloat16)
 
     barrier = pltpu.get_barrier_semaphore()
     for where in (dev(pp=1 - p), dev(pp=1 - p, ff=1 - f), dev(ff=1 - f), dev(xx=1 - x)):
@@ -115,71 +119,84 @@
             barrier, inc=1, device_id=dev(zz=z + 1), device_id_type=pl.DeviceIdType.MESH
         )
 
+    scale(coef_a, eig_a, 0)
+    scale(coef_g, eig_g, rows_a)
     pl.semaphore_wait(barrier, 4 + jnp.where(z > 0, 1, 0) + jnp.where(z < nz - 1, 1, 0))
-    own.wait()
-
-    def line(block, ss, rr, up, step):
+
+    def line(block, ss, rr, up, step, h):
         zb = z - (step - 1) if up else z + (step - 1)
         k = 0 if up else 1
-        return send(block(zb, x), block(zb, x), ss.at[k, step], rr.at[k, step],
+        return send(block(zb, x, h), block(zb, x, h), ss.at[k, step, h], rr.at[k, step, h],
                     dev(zz=z + 1 if up else z - 1))
 
-    def landed(block, ss, rr, up, step):
+    def landed(block, ss, rr, up, step, h):
         zb = z - step if up else z + step
         k = 0 if up else 1
-        return send(block(zb, x), block(zb, x), ss.at[k, step], rr.at[k, step],
+        return send(block(zb, x, h), block(zb, x, h), ss.at[k, step, h], rr.at[k, step, h],
                     dev(zz=z - 1 if up else z + 1))
 
-    def across(block, ss, rr, zb, xb):
-        return send(block(zb, xb), block(zb, xb), ss.at[zb], rr.at[zb], dev(xx=1 - x))
-
-    def twin(zb, xb, ff):
-        return send(coefs.at[zb, xb, ff], coefs.at[zb, xb, ff],
-                    sib_s.at[zb, xb], sib_r.at[zb, xb], dev(ff=1 - f))
-
-    def gather(block, ls, lr, xs, xr, extra, use):
-        def pass_on(zb):
-            across(block, xs, xr, zb, x).start()
-            extra(zb, x)
-
-        @pl.when(z < nz - 1)
-        def _():
-            line(block, ls, lr, True, 1).start()
-
-        @pl.when(z > 0)
-        def _():
-            line(block, ls, lr, False, 1).start()
-
-        pass_on(z)
+    def across(block, ss, rr, zb, xb, h):
+        return send(block(zb, xb, h), block(zb, xb, h), ss.at[zb, h], rr.at[zb, h],
+                    dev(xx=1 - x))
+
+    def block1(zb, xb, h, ff=None):
+        chunk = (rows_a + rows_g) // 2
+        return coefs.at[zb, xb, f if ff is None else ff, pl.ds(h * chunk, chunk)]
+
+    def twin(zb, xb, ff, h):
+        return send(block1(zb, xb, h, ff), block1(zb, xb, h, ff),
+                    sib_s.at[zb, xb, h], sib_r.at[zb, xb, h], dev(ff=1 - f))
+
+    def gather(block, ls, lr, xs, xr, extra, use, between):
+        def pass_on(zb, h):
+            across(block, xs, xr, zb, x, h).start()
+            extra(zb, x, h)
+
+        def begin(h):
+            @pl.when(z < nz - 1)
+            def _():
+                line(block, ls, lr, True, 1, h).start()
+
+            @pl.when(z > 0)
+            def _():
+                line(block, ls, lr, False, 1, h).start()
+
+            pass_on(z, h)
+
+        begin(0)
+        between()
+        begin(1)
 
         def step(s, carry):
-            @pl.when((s < nz) & (z - s >= 0))
-            def _():
-                landed(block, ls, lr, True, s).wait_recv()
-
-                @pl.when(z < nz - 1)
+            for h in range(2):
+                @pl.when((s < nz) & (z - s >= 0))
                 def _():
-                    line(block, ls, lr, True, s + 1).start()
-
-                pass_on(z - s)
-
-            @pl.when((s < nz) & (z + s < nz))
-            def _():
-                landed(block, ls, lr, False, s).wait_recv()
-
-                @pl.when(z > 0)
+                    landed(block, ls, lr, True, s, h).wait_recv()
+
+                    @pl.when(z < nz - 1)
+                    def _():
+                        line(block, ls, lr, True, s + 1, h).start()
+
+                    pass_on(z - s, h)
+
+                @pl.when((s < nz) & (z + s < nz))
                 def _():
-                    line(block, ls, lr, False, s + 1).start()
-
-                pass_on(z + s)
+                    landed(block, ls, lr, False, s, h).wait_recv()
+
+                    @pl.when(z > 0)
+                    def _():
+                        line(block, ls, lr, False, s + 1, h).start()
+
+                    pass_on(z + s, h)
 
             def side(j, c):
                 zb = z + (s - 1) * (2 * j - 1)
 
                 @pl.when((zb >= 0) & (zb < nz) & ((s > 1) | (j == 0)))
                 def _():
-                    across(block, xs, xr, zb, 1 - x).wait_recv()
-                    extra(zb, 1 - x)
+                    for h in range(2):
+                        across(block, xs, xr, zb, 1 - x, h).wait_recv()
+                        extra(zb, 1 - x, h)
                     use(zb)
 
                 return c
@@ -190,20 +207,22 @@
 
     def gather_sent(block, ls, lr, xs, xr):
         def step(s, carry):
-            @pl.when((z < nz - 1) & (z - s + 1 >= 0))
-            def _():
-                line(block, ls, lr, True, s).wait_send()
-
-            @pl.when((z > 0) & (z + s - 1 < nz))
-            def _():
-                line(block, ls, lr, False, s).wait_send()
+            for h in range(2):
+                @pl.when((z < nz - 1) & (z - s + 1 >= 0))
+                def _():
+                    line(block, ls, lr, True, s, h).wait_send()
+
+                @pl.when((z > 0) & (z + s - 1 < nz))
+                def _():
+                    line(block, ls, lr, False, s, h).wait_send()
 
             return carry
 
         lax.fori_loop(1, nz, step, 0)
 
         def crossing(zb, carry):
-            across(block, xs, xr, zb, x).wait_send()
+            for h in range(2):
+                across(block, xs, xr, zb, x, h).wait_send()
             return carry
 
         lax.fori_loop(0, nz, crossing, 0)
@@ -230,21 +249,20 @@
         return send(grads.at[:, cols_g(db, 1 - p)], toks_g.at[q, db], tg_s.at[db], tg_r.at[db],
                     dev(pp=1 - p))
 
-    early = (nd + 1) // 2
+    early = nd - nx
 
     def start_swaps(lo, hi):
-        def body(db, carry):
+        def body(i, carry):
+            near = jnp.where(2 * z < nz, z + i // nx, z + nz - i // nx)
+            db = lax.rem(near, nz) * nx + i % nx
             swap_a(db, p).start()
             swap_g(db, p).start()
             return carry
 
         lax.fori_loop(lo, hi, body, 0)
 
-    def block1(zb, xb):
-        return coefs.at[zb, xb, f]
-
-    def extra1(zb, xb):
-        twin(zb, xb, f).start()
+    def extra1(zb, xb, h):
+        twin(zb, xb, f, h).start()
 
     sum_a[...] = jnp.zeros_like(sum_a)
     sum_g[...] = jnp.zeros_like(sum_g)
@@ -259,7 +277,8 @@
             load_g.wait()
 
         for xb in range(nx):
-            twin(zb, xb, 1 - f).wait_recv()
+            for h in range(2):
+                twin(zb, xb, 1 - f, h).wait_recv()
         total_a, total_g = sum_a[...], sum_g[...]
         for i in range(nx * 2):
             block = coefs.at[zb, i // 2, i % 2]
@@ -283,7 +302,7 @@
         return carry
 
     lax.fori_loop(0, nd, start_own, 0)
-    gather(block1, line1_s, line1_r, x1_s, x1_r, extra1, use1)
+    gather(block1, line1_s, line1_r, x1_s, x1_r, extra1, use1, lambda: None)
 
     def halves(q):
         return (
@@ -299,10 +318,12 @@
     facs[z, x, p, :half_a] = keep_a
     facs[z, x, p, half_a:] = keep_g
     start_swaps(early, nd)
-    send(give, facs.at[z, x, 1 - p], y_s, y_r, dev(pp=1 - p)).wait()
-
-    def block2(zb, xb):
-        return facs.at[zb, xb]
+
+    def block2(zb, xb, h):
+        return facs.at[zb, xb, p if h == 0 else 1 - p]
+
+    def between2():
+        send(give, facs.at[z, x, 1 - p], y_s, y_r, dev(pp=1 - p)).wait_recv()
 
     lead = half_a - step_a
 
@@ -322,7 +343,7 @@
                 proj[0, q] += jnp.dot(toks_a[q, db], fac_a, preferred_element_type=jnp.float32)
                 proj[1, q] += jnp.dot(toks_g[q, db], fac_g, preferred_element_type=jnp.float32)
 
-    gather(block2, line2_s, line2_r, x2_s, x2_r, lambda zb, xb: None, use2)
+    gather(block2, line2_s, line2_r, x2_s, x2_r, lambda zb, xb, h: None, use2, between2)
 
     def half(q):
         return pl.ds(pl.multiple_of(q * LANES, LANES), LANES)
@@ -370,7 +391,8 @@
     gather_sent(block2, line2_s, line2_r, x2_s, x2_r)
 
     def twins(db, carry):
-        twin(db // nx, db % nx, f).wait_send()
+        for h in range(2):
+            twin(db // nx, db % nx, f, h).wait_send()
         return carry
 
     lax.fori_loop(0, nd, twins, 0)
@@ -381,12 +403,12 @@
         return carry
 
     lax.fori_loop(0, nd, swaps, 0)
+    send(give, facs.at[z, x, p], y_s, y_r, dev(pp=1 - p)).wait_send()
     for copy in ends:
         copy.wait_send()
 
 
 def with_kernel(nz, nx, acts, grads, lengths, basis_a, basis_g, coef_a, coef_g, eig_a, eig_g):
-    stack = jnp.concatenate([scaled(coef_a, eig_a), scaled(coef_g, eig_g)], axis=0)
     rows_a, rows_g = basis_a.shape[1], basis_g.shape[1]
     tok_rows, docs = acts.shape[0], lengths.shape[1]
     nd = nz * nx
@@ -400,7 +422,7 @@
         functools.partial(kernel, (nz, nx, rows_a, rows_g, docs)),
         out_shape=jax.ShapeDtypeStruct((docs, owned), f32),
         in_specs=[
-            pl.BlockSpec(memory_space=pltpu.SMEM), pl.BlockSpec(memory_space=vmem),
+            pl.BlockSpec(memory_space=pltpu.SMEM), *[pl.BlockSpec(memory_space=vmem)] * 4,
             anywhere, anywhere, anywhere, anywhere,
         ],
         out_specs=pl.BlockSpec(memory_space=vmem),
@@ -419,9 +441,10 @@
             vmem((2, tok_rows, LANES), f32),
             vmem((2, 2, tok_rows, LANES), bf),
             vmem((2, 2, tok_rows, LANES), bf),
-            dma((nz,)), dma, dma,
-            dma((2, nz + 1)), dma((2, nz + 1)), dma((nz,)), dma((nz,)), dma((nz, nx)), dma((nz, nx)),
-            dma((2, nz + 1)), dma((2, nz + 1)), dma((nz,)), dma((nz,)), dma, dma,
+            dma((nz,)), dma,
+            dma((2, nz + 1, 2)), dma((2, nz + 1, 2)), dma((nz, 2)), dma((nz, 2)),
+            dma((nz, nx, 2)), dma((nz, nx, 2)),
+            dma((2, nz + 1, 2)), dma((2, nz + 1, 2)), dma((nz, 2)), dma((nz, 2)), dma, dma,
             dma((nd,)), dma((nd,)), dma((nd,)), dma((nd,)), dma((nd,)), dma((nd,)),
             dma((3,)), dma((3,)),
         ],
@@ -432,7 +455,7 @@
             flops=2 * rows_a * basis_a.shape[2] * LANES, transcendentals=0,
             bytes_accessed=2 * basis_a.size,
         ),
-    )(lengths, stack, acts, grads, basis_a, basis_g)
+    )(lengths, coef_a, coef_g, eig_a, eig_g, acts, grads, basis_a, basis_g)
 
 
 def chosen(sizes, *arrays):

time: 88.3 us -> 74.4 us (0.84)
  Pallas kernels: 82.3 us -> 73 us
  other arithmetic: 4.43 us -> 0 us
    pallas_call x1, Pallas kernels: 82.3 us -> 73 us  [with_kernel(): pl.pallas_call(functools.partial(kernel, (nz, nx, rows_a, rows_g, docs)),...]
    convert_element_type x2 -> x0, other arithmetic: 2.22 us -> none  [scaled(): (coef.astype(jnp.float32) / (eig[:, None] + damping)).astype(jnp.bfloat16)]
    add x2 -> x0, other arithmetic: 1.37 us -> none  [scaled(): eig[:, None] + damping]
where the time goes in v2:
time: 74.4 us; the launch traced here: 74.2 us
  Pallas kernels  73 us (98%)
  local copies, waits for them, and re-layouts  1.26 us (2%)
    pallas_call x1, Pallas kernels, with_kernel(): pl.pallas_call(functools.partial(kernel, (nz, nx, rows_a, rows_g, docs)),...  73 us

profile of v2, /device:TPU:1, one launch (start us, length us, event | category | flops | bytes accessed | tf_op | source)
XLA Modules:
  0.0 74.2 jit_solution(8897160197158210443)
XLA Ops:
  0.0 73.0 %shard_map.91 = f32[4,4]{1,0:T(4,128)} custom-call(s32[1,4]{1,0:T(1,128)} %len_ref.1, bf16[896,256]{1,0:T(8,128)(2,1)} %coef_a.1, bf16[256,256]{1,0:T(8,128)(2,1)} %coef_g.1, f32[896]{0:T(1024)} %eig_a.1, f32[256]{0:T(256)} %eig_g.1, bf16[176,7168]{1,0:T(8,128)(2,1)} %acts.1, bf16[176,2048]{1,0:T(8,128)(2,1)} %grads.1, bf16[1,896,14336]{2,1,0:T(8,128)(2,1)} %basis_a.1, ...), custom_call_target="tpu_custom_call" | custom-call | flops 3288334336 | bytes 25690112 | tf_op jit(solution)/shard_map/pallas_call | solution.py:421
  73.0 1.3 %copy.11 = f32[4,4]{1,0:T(4,128)} copy(f32[4,4]{1,0:T(4,128)} %shard_map.91) | data formatting | bytes 128
